TPU v7x, 32 devices: a whole 2x2x4 slice. The times are simulated.
32 devices in a mesh: ctx: 8 (over y, x, core), fsdp: 4 (over z).
Axes of the slice: x: 2, y: 2, z: 4, core: 2. Of those that a mesh axis runs over, the one named last changes fastest.
Arguments:
- layer_input: bfloat16 [4, 1024, 768], P('fsdp', 'ctx'), may hold values from -6 to 6
- qkv_weight: bfloat16 [768, 2304], P('fsdp'), may hold values from -0.21875 to 0.21875
- query_bias: bfloat16 [768], P('fsdp'), may hold values from -1.5 to 1.5
- value_bias: bfloat16 [768], P('fsdp'), may hold values from -1.5 to 1.5
- out_weight: bfloat16 [768, 768], P('fsdp'), may hold values from -0.875 to 0.875
- out_bias: bfloat16 [768], P('fsdp'), may hold values from -2.5 to 2.5
- first_gain: bfloat16 [768], P('fsdp'), may hold values from 0.25 to 1.75
- first_shift: bfloat16 [768], P('fsdp'), may hold values from -1.5 to 1.5
- second_gain: bfloat16 [768], P('fsdp'), may hold values from 0.25 to 1.75
- second_shift: bfloat16 [768], P('fsdp'), may hold values from -1.5 to 1.5
- up_weight: bfloat16 [768, 3072], P('fsdp'), may hold values from -0.21875 to 0.21875
- up_bias: bfloat16 [3072], P('fsdp'), may hold values from -2.5 to 2.5
- down_weight: bfloat16 [3072, 768], P('fsdp'), may hold values from -0.109375 to 0.109375
- down_bias: bfloat16 [768], P('fsdp'), may hold values from -2.5 to 2.5
- out_grad: bfloat16 [4, 1024, 768], P('fsdp', 'ctx'), may hold values from -6 to 6
Outputs:
- layer_output: bfloat16 [4, 1024, 768], P('fsdp', 'ctx')
- input_grad: float32 [4, 1024, 768], P('fsdp', 'ctx')
- qkv_weight_grad: float32 [768, 2304], P('fsdp')
- query_bias_grad: float32 [768], P('fsdp')
- value_bias_grad: float32 [768], P('fsdp')
- out_weight_grad: float32 [768, 768], P('fsdp')
- out_bias_grad: float32 [768], P('fsdp')
- first_gain_grad: float32 [768], P('fsdp')
- first_shift_grad: float32 [768], P('fsdp')
- second_gain_grad: float32 [768], P('fsdp')
- second_shift_grad: float32 [768], P('fsdp')
- up_weight_grad: float32 [768, 3072], P('fsdp')
- up_bias_grad: float32 [3072], P('fsdp')
- down_weight_grad: float32 [3072, 768], P('fsdp')
- down_bias_grad: float32 [768], P('fsdp')
All inputs are finite; a program needn't handle non-finite values.
Results may differ from a plain program's by a relative error of at most 0.018.
Values may be sent and summed in bfloat16 or wider, within the bound.
A program may use at most 128 MiB of HBM per device.

v0:
```python
import math

import jax
import jax.numpy as jnp
from jax import lax
from jax.sharding import PartitionSpec as P

HD = 64


EPS = 1e-05
NEG = -1e30
GELU_C = 0.7978845608028654
GELU_A = 0.044715


def gelu_pair(values):
    inner = GELU_C * (values + GELU_A * values * values * values)
    tanh_val = jnp.tanh(inner)
    result = 0.5 * values * (1.0 + tanh_val)
    slope = 0.5 * (1.0 + tanh_val) + 0.5 * values * (1.0 - tanh_val * tanh_val) * GELU_C * (
        1.0 + 3.0 * GELU_A * values * values
    )
    return (result, slope)


def norm_rows(values, gain, shift):
    mean = jnp.mean(values, axis=-1, keepdims=True)
    centred = values - mean
    inv_std = lax.rsqrt(jnp.mean(centred * centred, axis=-1, keepdims=True) + EPS)
    normed = centred * inv_std
    return (normed * gain.astype(jnp.float32) + shift.astype(jnp.float32), normed, inv_std)


def norm_back(grad_out, normed, inv_std, gain):
    scaled = grad_out * gain.astype(jnp.float32)
    return inv_std * (
        scaled
        - jnp.mean(scaled, axis=-1, keepdims=True)
        - normed * jnp.mean(scaled * normed, axis=-1, keepdims=True)
    )


def matmul(left, right):
    return jnp.dot(left, right, preferred_element_type=jnp.float32)


def inner_rows(left, right):
    return lax.dot_general(
        left, right, (((0,), (0,)), ((), ())), preferred_element_type=jnp.float32
    )


def outer_cols(left, right):
    return lax.dot_general(
        left, right, (((1,), (1,)), ((), ())), preferred_element_type=jnp.float32
    )


def fold_keys(queries, positions, scale):

    def step(carry, pieces, start):
        top, total, accum = carry
        keys, values = pieces
        scores = (
            jnp.einsum("sqhd,skhd->shqk", queries, keys, preferred_element_type=jnp.float32) * scale
        )
        key_pos = jnp.arange(keys.shape[1], dtype=jnp.int32)
        causal = (key_pos[None, :] <= positions[:, None])[None, None]
        masked = jnp.where(causal, scores, NEG)
        new_top = jnp.maximum(top, jnp.max(masked, axis=-1))
        factor = jnp.exp(top - new_top)
        weights = jnp.where(causal, jnp.exp(masked - new_top[..., None]), 0.0)
        total = jnp.sum(weights, axis=-1)
        accum = jnp.einsum(
            "shqk,skhd->shqd",
            weights,
            values.astype(jnp.float32),
            precision=lax.Precision.HIGHEST,
            preferred_element_type=jnp.float32,
        )
        return (new_top, total, accum)

    return step


def span_count(block, span):
    return ((lax.axis_index("ctx") + 1) * block + span - 1) // span


def attend_back(queries, keys_all, values_all, grad_heads, logsum, delta, positions, scale, block):
    length = keys_all.shape[1]
    span = min(512, length)

    def visit(index, carry):
        grad_query, grad_keys, grad_values = carry
        start = index * span
        keys = lax.dynamic_slice_in_dim(keys_all, start, span, 1)
        values = lax.dynamic_slice_in_dim(values_all, start, span, 1)
        scores = (
            jnp.einsum("sqhd,skhd->shqk", queries, keys, preferred_element_type=jnp.float32) * scale
        )
        key_pos = start + jnp.arange(span, dtype=jnp.int32)
        causal = (key_pos[None, :] <= positions[:, None])[None, None]
        probs = jnp.where(causal, jnp.exp(scores - logsum[..., None]), 0.0)
        value_part = jnp.einsum(
            "shqk,sqhd->skhd",
            probs.astype(jnp.bfloat16),
            grad_heads,
            preferred_element_type=jnp.float32,
        )
        grad_probs = jnp.einsum(
            "sqhd,skhd->shqk", grad_heads, values, preferred_element_type=jnp.float32
        )
        grad_scores = (probs * (grad_probs - delta[..., None])).astype(jnp.bfloat16)
        grad_query = (
            grad_query
            + jnp.einsum("shqk,skhd->sqhd", grad_scores, keys, preferred_element_type=jnp.float32)
            * scale
        )
        key_part = (
            jnp.einsum("shqk,sqhd->skhd", grad_scores, queries, preferred_element_type=jnp.float32)
            * scale
        )
        grad_keys = lax.dynamic_update_slice_in_dim(grad_keys, key_part, start, 1)
        grad_values = lax.dynamic_update_slice_in_dim(grad_values, value_part, start, 1)
        return (grad_query, grad_keys, grad_values)

    start_state = (
        jnp.zeros(queries.shape, jnp.float32),
        jnp.zeros(keys_all.shape, jnp.float32),
        jnp.zeros(values_all.shape, jnp.float32),
    )
    return lax.fori_loop(0, span_count(block, span), visit, start_state)


def shards(
    layer_input,
    qkv_weight,
    query_bias,
    value_bias,
    out_weight,
    out_bias,
    first_gain,
    first_shift,
    second_gain,
    second_shift,
    up_weight,
    up_bias,
    down_weight,
    down_bias,
    out_grad,
):
    seqs, block, width = layer_input.shape
    rows = seqs * block
    heads = width // HD
    scale = 1.0 / math.sqrt(HD)
    shape_heads = (seqs, block, heads, HD)
    full = (
        lax.all_gather(qkv_weight, "fsdp", axis=0, tiled=True),
        lax.all_gather(query_bias, "fsdp", axis=0, tiled=True),
        lax.all_gather(value_bias, "fsdp", axis=0, tiled=True),
        lax.all_gather(out_weight, "fsdp", axis=0, tiled=True),
        lax.all_gather(out_bias, "fsdp", axis=0, tiled=True),
        lax.all_gather(first_gain, "fsdp", axis=0, tiled=True),
        lax.all_gather(first_shift, "fsdp", axis=0, tiled=True),
        lax.all_gather(second_gain, "fsdp", axis=0, tiled=True),
        lax.all_gather(second_shift, "fsdp", axis=0, tiled=True),
        lax.all_gather(up_weight, "fsdp", axis=0, tiled=True),
        lax.all_gather(up_bias, "fsdp", axis=0, tiled=True),
        lax.all_gather(down_weight, "fsdp", axis=0, tiled=True),
        lax.all_gather(down_bias, "fsdp", axis=0, tiled=True),
    )
    (
        qkv_matrix,
        query_shift,
        value_shift,
        out_matrix,
        out_shift,
        gain_one,
        shift_one,
        gain_two,
        shift_two,
        up_matrix,
        up_shift,
        down_matrix,
        down_shift,
    ) = full
    inputs = layer_input.reshape(rows, width).astype(jnp.float32)
    normed_one, unit_one, inv_one = norm_rows(inputs, gain_one, shift_one)
    mixed_in = normed_one.astype(jnp.bfloat16)
    projected = matmul(mixed_in, qkv_matrix)
    queries = (
        (projected[:, :width] + query_shift.astype(jnp.float32))
        .astype(jnp.bfloat16)
        .reshape(shape_heads)
    )
    keys_local = projected[:, width : 2 * width].astype(jnp.bfloat16).reshape(shape_heads)
    values_local = (
        (projected[:, 2 * width :] + value_shift.astype(jnp.float32))
        .astype(jnp.bfloat16)
        .reshape(shape_heads)
    )
    positions = lax.axis_index("ctx") * block + jnp.arange(block, dtype=jnp.int32)
    step = fold_keys(queries, positions, scale)
    start_state = (
        jnp.full((seqs, heads, block), NEG, jnp.float32),
        jnp.zeros((seqs, heads, block), jnp.float32),
        jnp.zeros((seqs, heads, block, HD), jnp.float32),
    )
    top, total, accum = step(
        start_state,
        (
            lax.all_gather(keys_local, "ctx", axis=1, tiled=True),
            lax.all_gather(values_local, "ctx", axis=1, tiled=True),
        ),
        jnp.int32(0),
    )
    attended = (
        (accum / total[..., None]).transpose(0, 2, 1, 3).reshape(rows, width).astype(jnp.bfloat16)
    )
    logsum = top + jnp.log(total)
    hidden = inputs + matmul(attended, out_matrix) + out_shift.astype(jnp.float32)
    normed_two, unit_two, inv_two = norm_rows(hidden, gain_two, shift_two)
    ffn_in = normed_two.astype(jnp.bfloat16)
    lifted = matmul(ffn_in, up_matrix) + up_shift.astype(jnp.float32)
    gelu_val, gelu_slope = gelu_pair(lifted)
    active = gelu_val.astype(jnp.bfloat16)
    result = hidden + matmul(active, down_matrix) + down_shift.astype(jnp.float32)
    layer_output = result.astype(jnp.bfloat16).reshape(seqs, block, width)
    again = (
        lax.all_gather(qkv_weight, "fsdp", axis=0, tiled=True),
        lax.all_gather(out_weight, "fsdp", axis=0, tiled=True),
        lax.all_gather(first_gain, "fsdp", axis=0, tiled=True),
        lax.all_gather(second_gain, "fsdp", axis=0, tiled=True),
        lax.all_gather(up_weight, "fsdp", axis=0, tiled=True),
        lax.all_gather(down_weight, "fsdp", axis=0, tiled=True),
    )
    qkv_matrix, out_matrix, gain_one, gain_two, up_matrix, down_matrix = again
    upstream = out_grad.reshape(rows, width)
    upstream_f = upstream.astype(jnp.float32)
    grad_down_shift = jnp.sum(upstream_f, axis=0)
    grad_down = inner_rows(active, upstream)
    grad_active = outer_cols(upstream, down_matrix)
    grad_lifted = grad_active * gelu_slope
    lifted_b = grad_lifted.astype(jnp.bfloat16)
    grad_up_shift = jnp.sum(grad_lifted, axis=0)
    grad_up = inner_rows(ffn_in, lifted_b)
    grad_normed_two = outer_cols(lifted_b, up_matrix)
    grad_gain_two = jnp.sum(grad_normed_two * unit_two, axis=0)
    grad_shift_two = jnp.sum(grad_normed_two, axis=0)
    grad_hidden = upstream_f + norm_back(grad_normed_two, unit_two, inv_two, gain_two)
    hidden_b = grad_hidden.astype(jnp.bfloat16)
    grad_out_shift = jnp.sum(grad_hidden, axis=0)
    grad_out = inner_rows(attended, hidden_b)
    grad_attended = outer_cols(hidden_b, out_matrix).astype(jnp.bfloat16)
    grad_heads = grad_attended.reshape(shape_heads)
    delta = jnp.sum(
        grad_heads.astype(jnp.float32) * attended.reshape(shape_heads).astype(jnp.float32), axis=-1
    ).transpose(0, 2, 1)
    keys_all, values_all = (
        lax.all_gather(keys_local, "ctx", axis=1, tiled=True),
        lax.all_gather(values_local, "ctx", axis=1, tiled=True),
    )
    grad_query, key_terms, value_terms = attend_back(
        queries, keys_all, values_all, grad_heads, logsum, delta, positions, scale, block
    )
    grad_keys, grad_values = (
        lax.psum_scatter(key_terms, "ctx", scatter_dimension=1, tiled=True),
        lax.psum_scatter(value_terms, "ctx", scatter_dimension=1, tiled=True),
    )
    query_rows = grad_query.reshape(rows, width)
    value_rows = grad_values.reshape(rows, width)
    grad_proj = jnp.concatenate([query_rows, grad_keys.reshape(rows, width), value_rows], axis=1)
    proj_b = grad_proj.astype(jnp.bfloat16)
    grad_qkv = inner_rows(mixed_in, proj_b)
    grad_query_shift = jnp.sum(query_rows, axis=0)
    grad_value_shift = jnp.sum(value_rows, axis=0)
    grad_normed_one = outer_cols(proj_b, qkv_matrix)
    grad_gain_one = jnp.sum(grad_normed_one * unit_one, axis=0)
    grad_shift_one = jnp.sum(grad_normed_one, axis=0)
    input_grad = (grad_hidden + norm_back(grad_normed_one, unit_one, inv_one, gain_one)).reshape(
        seqs, block, width
    )
    owned = (
        lax.psum_scatter(
            grad_qkv.astype(jnp.bfloat16), "fsdp", scatter_dimension=0, tiled=True
        ).astype(jnp.float32),
        lax.psum_scatter(
            grad_query_shift.astype(jnp.bfloat16), "fsdp", scatter_dimension=0, tiled=True
        ).astype(jnp.float32),
        lax.psum_scatter(
            grad_value_shift.astype(jnp.bfloat16), "fsdp", scatter_dimension=0, tiled=True
        ).astype(jnp.float32),
        lax.psum_scatter(
            grad_out.astype(jnp.bfloat16), "fsdp", scatter_dimension=0, tiled=True
        ).astype(jnp.float32),
        lax.psum_scatter(
            grad_out_shift.astype(jnp.bfloat16), "fsdp", scatter_dimension=0, tiled=True
        ).astype(jnp.float32),
        lax.psum_scatter(
            grad_gain_one.astype(jnp.bfloat16), "fsdp", scatter_dimension=0, tiled=True
        ).astype(jnp.float32),
        lax.psum_scatter(
            grad_shift_one.astype(jnp.bfloat16), "fsdp", scatter_dimension=0, tiled=True
        ).astype(jnp.float32),
        lax.psum_scatter(
            grad_gain_two.astype(jnp.bfloat16), "fsdp", scatter_dimension=0, tiled=True
        ).astype(jnp.float32),
        lax.psum_scatter(
            grad_shift_two.astype(jnp.bfloat16), "fsdp", scatter_dimension=0, tiled=True
        ).astype(jnp.float32),
        lax.psum_scatter(
            grad_up.astype(jnp.bfloat16), "fsdp", scatter_dimension=0, tiled=True
        ).astype(jnp.float32),
        lax.psum_scatter(
            grad_up_shift.astype(jnp.bfloat16), "fsdp", scatter_dimension=0, tiled=True
        ).astype(jnp.float32),
        lax.psum_scatter(
            grad_down.astype(jnp.bfloat16), "fsdp", scatter_dimension=0, tiled=True
        ).astype(jnp.float32),
        lax.psum_scatter(
            grad_down_shift.astype(jnp.bfloat16), "fsdp", scatter_dimension=0, tiled=True
        ).astype(jnp.float32),
    )
    summed = (
        lax.psum(owned[0].astype(jnp.bfloat16), "ctx").astype(jnp.float32),
        lax.psum(owned[1].astype(jnp.bfloat16), "ctx").astype(jnp.float32),
        lax.psum(owned[2].astype(jnp.bfloat16), "ctx").astype(jnp.float32),
        lax.psum(owned[3].astype(jnp.bfloat16), "ctx").astype(jnp.float32),
        lax.psum(owned[4].astype(jnp.bfloat16), "ctx").astype(jnp.float32),
        lax.psum(owned[5].astype(jnp.bfloat16), "ctx").astype(jnp.float32),
        lax.psum(owned[6].astype(jnp.bfloat16), "ctx").astype(jnp.float32),
        lax.psum(owned[7].astype(jnp.bfloat16), "ctx").astype(jnp.float32),
        lax.psum(owned[8].astype(jnp.bfloat16), "ctx").astype(jnp.float32),
        lax.psum(owned[9].astype(jnp.bfloat16), "ctx").astype(jnp.float32),
        lax.psum(owned[10].astype(jnp.bfloat16), "ctx").astype(jnp.float32),
        lax.psum(owned[11].astype(jnp.bfloat16), "ctx").astype(jnp.float32),
        lax.psum(owned[12].astype(jnp.bfloat16), "ctx").astype(jnp.float32),
    )
    return (
        layer_output,
        input_grad,
        summed[0],
        summed[1],
        summed[2],
        summed[3],
        summed[4],
        summed[5],
        summed[6],
        summed[7],
        summed[8],
        summed[9],
        summed[10],
        summed[11],
        summed[12],
    )


def solution(mesh):
    placed = (
        P("fsdp", "ctx", None),
        P("fsdp", None),
        P("fsdp"),
        P("fsdp"),
        P("fsdp", None),
        P("fsdp"),
        P("fsdp"),
        P("fsdp"),
        P("fsdp"),
        P("fsdp"),
        P("fsdp", None),
        P("fsdp"),
        P("fsdp", None),
        P("fsdp"),
        P("fsdp", "ctx", None),
    )
    return jax.shard_map(
        shards,
        mesh=mesh,
        in_specs=placed,
        out_specs=(
            P("fsdp", "ctx", None),
            P("fsdp", "ctx", None),
            P("fsdp", None),
            P("fsdp"),
            P("fsdp"),
            P("fsdp", None),
            P("fsdp"),
            P("fsdp"),
            P("fsdp"),
            P("fsdp"),
            P("fsdp"),
            P("fsdp", None),
            P("fsdp"),
            P("fsdp", None),
            P("fsdp"),
        ),
        check_vma=False,
    )
```

profile of v0, /device:TPU:0, one launch (start us, length us, event | category | flops | bytes accessed | tf_op | source)
XLA Modules:
  0.0 846.6 jit_solution(3731395561872152435)
XLA Ops:
  8.0 1.3 fusion.93
  15.8 21.3 %all-reduce.20 = (bf16[768]{0:T(1024)(128)(2,1)S(1)}, bf16[768]{0:T(1024)(128)(2,1)S(1)}, bf16[768]{0:T(1024)(128)(2,1)S(1)}, bf16[768]{0:T(1024)(128)(2,1)S(1)}...) all-reduce(bf16[768]{0:T(1024)(128)(2,1)S(1)} %dynamic-update-slice, ...), channel_id=1, replica_groups=mesh['ctx'=8,'fsdp'=4] {'fsdp'}, use_global_device_ids=true, to_apply=%add.1 | all-reduce | flops 5376 | bytes 21504
  38.1 1.1 fusion.71
  39.3 43.2 %all-gather.8.cloned.1.call-done = bf16[768,2304]{1,0:T(8,128)(2,1)} async-done(((bf16[192,2304]{1,0:T(8,128)(2,1)}), bf16[768,2304]{1,0:T(8,128)(2,1)}) %all-gather.8.cloned.1.call-update) | async-done | bytes 3538960 | tf_op jit(solution)/shard_map/all_gather | solution.py:160
  82.5 2.8 fusion.88
  89.1 13.0 %all-gather = bf16[4,1,768]{2,1,0:T(2,128)(2,1)S(1)} all-gather(bf16[1,1,768]{2,1,0:T(2,128)(2,1)S(1)} %reshape.336), channel_id=1, replica_groups=mesh['ctx'=8,'fsdp'=4] {'fsdp'}, dimensions={0}, use_global_device_ids=true | all-gather | bytes 7680 | tf_op jit(solution)/shard_map/all_gather | solution.py:170
  102.5 8.5 %all-gather.10.cloned.1.call-done = bf16[1,1024,12,64]{1,3,2,0:T(8,128)(2,1)} async-done(((bf16[1,128,12,64]{1,3,2,0:T(8,128)(2,1)}), bf16[1,1024,12,64]{1,3,2,0:T(8,128)(2,1)}) %all-gather.10.cloned.1.call-update) | async-done | bytes 1572880 | tf_op jit(solution)/shard_map/all_gather | solution.py:214
  110.9 2.7 fusion.30
  113.6 2.6 copy-done.1
  116.3 2.0 fusion.31
  118.3 21.0 %all-gather.12.cloned.1.call-done = bf16[1,1024,12,64]{1,3,2,0:T(8,128)(2,1)} async-done(((bf16[1,128,12,64]{1,3,2,0:T(8,128)(2,1)}), bf16[1,1024,12,64]{1,3,2,0:T(8,128)(2,1)}) %all-gather.12.cloned.1.call-update) | async-done | bytes 1572880 | tf_op jit(solution)/shard_map/all_gather | solution.py:215
  139.3 8.3 fusion.53
  147.6 23.6 %all-gather.14.cloned.1.call-done = bf16[768,768]{1,0:T(8,128)(2,1)} async-done(((bf16[192,768]{1,0:T(8,128)(2,1)}), bf16[768,768]{1,0:T(8,128)(2,1)}) %all-gather.14.cloned.1.call-update) | async-done | bytes 1179664 | tf_op jit(solution)/shard_map/all_gather | solution.py:163
  171.2 1.7 fusion.94
  173.8 87.4 %all-gather.16.cloned.1.call-done = bf16[768,3072]{1,0:T(8,128)(2,1)} async-done(((bf16[192,3072]{1,0:T(8,128)(2,1)}), bf16[768,3072]{1,0:T(8,128)(2,1)}) %all-gather.16.cloned.1.call-update) | async-done | bytes 4718608 | tf_op jit(solution)/shard_map/all_gather | solution.py:169
  261.2 3.2 convolution_add_fusion
  264.4 86.1 %all-gather.18.cloned.1.call-done = bf16[3072,768]{1,0:T(8,128)(2,1)} async-done(((bf16[768,768]{1,0:T(8,128)(2,1)}), bf16[3072,768]{1,0:T(8,128)(2,1)}) %all-gather.18.cloned.1.call-update) | async-done | bytes 4718608 | tf_op jit(solution)/shard_map/all_gather | solution.py:171
  350.5 4.9 fusion.95
  355.5 2.3 multiply_reduce_fusion
  357.8 1.6 fusion.90
  360.8 2.1 broadcast.184
  362.9 2.1 broadcast.184.clone
  365.0 9.8 %while.15 = (s32[]{:T(128)}, f32[1,128,12,64]{1,3,2,0:T(8,128)S(1)}, f32[1,1024,12,64]{1,3,2,0:T(8,128)}, f32[1,1024,12,64]{1,3,2,0:T(8,128)}, s32[]{:T(128)}, /...) while((s32[]{:T(128)}, ...), condition=%wide.region_10.11_spmd.clone, body=%wide.region_9.10_spmd.clone.sunk | while | flops 511836800 | bytes 78919112 | solution.py:134
  366.5 1.3 fusion.135
  368.4 1.4 copy-done.3
  370.4 1.9 copy-done.5
  373.1 1.7 copy-done.6
  375.6 1.5 convolution_convert_fusion.3
  377.2 3.6 convolution_convert_fusion.1
  380.9 1.3 copy-done.8
  382.2 3.8 convolution_convert_fusion
  386.3 43.0 %reduce-scatter.7.cloned.1.call-done = f32[1,128,12,64]{1,3,2,0:T(8,128)} async-done(((f32[1,1024,12,64]{1,3,2,0:T(8,128)}), f32[1,128,12,64]{1,3,2,0:T(8,128)}) %reduce-scatter.7.cloned.1.call-update) | async-done | bytes 393232 | tf_op jit(solution)/shard_map/reduce_scatter | solution.py:269
  430.4 49.0 %reduce-scatter.9.cloned.1.call-done = f32[1,128,12,64]{1,3,2,0:T(8,128)} async-done(((f32[1,1024,12,64]{1,3,2,0:T(8,128)}), f32[1,128,12,64]{1,3,2,0:T(8,128)}) %reduce-scatter.9.cloned.1.call-update) | async-done | bytes 393232 | tf_op jit(solution)/shard_map/reduce_scatter | solution.py:270
  479.4 1.3 fusion.92
  480.7 3.7 convolution_convert_fusion.2
  484.5 27.0 %reduce-scatter.13.cloned.1.call-done = bf16[192,768]{1,0:T(8,128)(2,1)} async-done(((bf16[768,768]{1,0:T(8,128)(2,1)}), bf16[192,768]{1,0:T(8,128)(2,1)}) %reduce-scatter.13.cloned.1.call-update) | async-done | bytes 294928 | tf_op jit(solution)/shard_map/reduce_scatter | solution.py:295
  511.5 86.1 %reduce-scatter.15.cloned.1.call-done = bf16[192,3072]{1,0:T(8,128)(2,1)} async-done(((bf16[768,3072]{1,0:T(8,128)(2,1)}), bf16[192,3072]{1,0:T(8,128)(2,1)}) %reduce-scatter.15.cloned.1.call-update) | async-done | bytes 1179664 | tf_op jit(solution)/shard_map/reduce_scatter | solution.py:313
  597.7 88.1 %reduce-scatter.17.cloned.1.call-done = bf16[768,768]{1,0:T(8,128)(2,1)} async-done(((bf16[3072,768]{1,0:T(8,128)(2,1)}), bf16[768,768]{1,0:T(8,128)(2,1)}) %reduce-scatter.17.cloned.1.call-update) | async-done | bytes 1179664 | tf_op jit(solution)/shard_map/reduce_scatter | solution.py:319
  685.8 69.1 %reduce-scatter.11.cloned.1.call-done = bf16[192,2304]{1,0:T(8,128)(2,1)} async-done(((bf16[768,2304]{1,0:T(8,128)(2,1)}), bf16[192,2304]{1,0:T(8,128)(2,1)}) %reduce-scatter.11.cloned.1.call-update) | async-done | bytes 884752 | tf_op jit(solution)/shard_map/reduce_scatter | solution.py:286
  756.7 4.1 fusion.70
  760.8 18.0 %all-reduce.19 = (bf16[768]{0:T(1024)(128)(2,1)S(1)}, bf16[768]{0:T(1024)(128)(2,1)S(1)}, bf16[768]{0:T(1024)(128)(2,1)S(1)}, bf16[768]{0:T(1024)(128)(2,1)S(1)}...) all-reduce(bf16[768]{0:T(1024)(128)(2,1)S(1)} %dynamic-update-slice, ...), channel_id=1, replica_groups=mesh['ctx'=8,'fsdp'=4] {'fsdp'}, use_global_device_ids=true, to_apply=%add.7 | all-reduce | flops 9984 | bytes 39936
  779.5 12.2 %all-reduce.17 = (bf16[192]{0:T(256)(128)(2,1)S(1)}, bf16[192]{0:T(256)(128)(2,1)S(1)}, bf16[192]{0:T(256)(128)(2,1)S(1)}, bf16[192]{0:T(256)(128)(2,1)S(1)}, bf...) all-reduce(bf16[192]{0:T(256)(128)(2,1)S(1)} %dynamic-slice.9, ...), channel_id=1, replica_groups=mesh['ctx'=8,'fsdp'=4] {'ctx'}, use_global_device_ids=true, to_apply=%region_19.20 | all-reduce | flops 2304 | bytes 9216 | tf_op jit(solution)/shard_map/psum | solution.py:328
  796.8 1.9 fusion.69
  798.7 4.1 fusion.49
  802.8 30.5 %all-reduce.23.cloned.1.call-done = (bf16[192,2304]{1,0:T(8,128)(2,1)}, bf16[192,768]{1,0:T(8,128)(2,1)}, bf16[192,3072]{1,0:T(8,128)(2,1)}, bf16[768,768]{1,0:T(8,128)(2,1)}) async-done(((bf16[192,2304]{1,0:T(8,128)(2,1)}, bf16[192,768]{1,0:T(8,128)(2,1)}, bf16[192,3072]{1,0:T(8,128)(2,1)}, bf16[768,768]{1,0:T(8,128)(2,1)}), (bf16[192,2304]{1,0:T(8,128)(2,1)}, bf16[192,768]{1,0:T(8,128)(2,1)}, ...) | async-done | bytes 3538960 | tf_op jit(solution)/shard_map/psum | solution.py:327
  833.4 2.6 convert_element_type.246
  836.8 1.7 convert_element_type.266
  838.5 1.6 convert_element_type.270
  (172 shorter events, 26.7 us)
Async XLA Ops:
  7.2 75.3 %all-gather.8.cloned.1.call-start = ((), (), s32[]{:S(2)}) async-start(), calls=%async_computation.6 | async-start | bytes 4423680 | tf_op jit(solution)/shard_map/all_gather | solution.py:160
  7.9 103.0 %all-gather.10.cloned.1.call-start = ((), (), s32[]{:S(2)}) async-start(), calls=%async_computation.7 | async-start | bytes 1769472 | tf_op jit(solution)/shard_map/all_gather | solution.py:214
  38.1 47.2 %copy-start.23 = (f32[128]{0:T(128)}, f32[128]{0:T(128)S(1)}, u32[]{:S(2)}) copy-start(f32[128]{0:T(128)S(1)} %broadcast_multiply_fusion.5) | copy-start | bytes 1540
  39.3 43.3 %copy-start.30 = (f32[128]{0:T(128)}, f32[128]{0:T(128)S(1)}, u32[]{:S(2)}) copy-start(f32[128]{0:T(128)S(1)} %add_rsqrt_fusion.1) | copy-start | bytes 1540
  86.2 53.1 %all-gather.12.cloned.1.call-start = ((), (), s32[]{:S(2)}) async-start(), calls=%async_computation.8 | async-start | bytes 1769472 | tf_op jit(solution)/shard_map/all_gather | solution.py:215
  86.4 2.7 copy-start.33
  87.2 84.0 %all-gather.14.cloned.1.call-start = ((), (), s32[]{:S(2)}) async-start(), calls=%async_computation.9 | async-start | bytes 1474560 | tf_op jit(solution)/shard_map/all_gather | solution.py:163
  87.8 173.4 %all-gather.16.cloned.1.call-start = ((), (), s32[]{:S(2)}) async-start(), calls=%async_computation.10 | async-start | bytes 5898240 | tf_op jit(solution)/shard_map/all_gather | solution.py:169
  88.4 262.1 %all-gather.18.cloned.1.call-start = ((), (), s32[]{:S(2)}) async-start(), calls=%async_computation.11 | async-start | bytes 5898240 | tf_op jit(solution)/shard_map/all_gather | solution.py:171
  89.0 340.4 %reduce-scatter.7.cloned.1.call-start = ((), (), s32[]{:S(2)}) async-start(), calls=%async_computation.12 | async-start | bytes 3538944 | tf_op jit(solution)/shard_map/reduce_scatter | solution.py:269
  113.6 2.7 copy-start.1
  118.2 53.0 %copy-start.9 = (bf16[1,128,768]{2,1,0:T(8,128)(2,1)S(1)}, bf16[1,128,768]{2,1,0:T(8,128)(2,1)}, u32[]{:S(2)}) copy-start(bf16[1,128,768]{2,1,0:T(8,128)(2,1)} %param.17) | copy-start | bytes 589828
  172.9 182.5 %copy-start.19 = (f32[128]{0:T(128)}, f32[128]{0:T(128)S(1)}, u32[]{:S(2)}) copy-start(f32[128]{0:T(128)S(1)} %broadcast_multiply_fusion.4) | copy-start | bytes 1540
  173.1 182.3 %copy-start.21 = (f32[128]{0:T(128)}, f32[128]{0:T(128)S(1)}, u32[]{:S(2)}) copy-start(f32[128]{0:T(128)S(1)} %add_rsqrt_fusion) | copy-start | bytes 1540
  261.2 89.3 %copy-start.13 = (bf16[1,128,768]{2,1,0:T(8,128)(2,1)S(1)}, bf16[1,128,768]{2,1,0:T(8,128)(2,1)}, u32[]{:S(2)}) copy-start(bf16[1,128,768]{2,1,0:T(8,128)(2,1)} %param.31) | copy-start | bytes 589828
  264.4 91.0 %copy-start.7 = (f32[128,3072]{1,0:T(8,128)}, f32[128,3072]{1,0:T(8,128)S(1)}, u32[]{:S(2)}) copy-start(f32[128,3072]{1,0:T(8,128)S(1)} %convolution_add_fusion) | copy-start | bytes 4718596
  350.5 4.9 copy-start.2
  355.4 2.3 copy-start.11
  357.8 1.6 copy-start.10
  362.9 2.1 copy-start
  365.0 0.9 copy-start.17
  365.0 0.9 copy-start.28
  365.0 0.9 copy-start.29
  365.0 1.5 copy-start.34
  367.8 1.9 copy-start.3
  369.7 2.5 copy-start.5
  370.4 2.6 copy-start.4
  373.1 1.7 copy-start.6
  374.8 104.6 %reduce-scatter.9.cloned.1.call-start = ((), (), s32[]{:S(2)}) async-start(), calls=%async_computation.13 | async-start | bytes 3538944 | tf_op jit(solution)/shard_map/reduce_scatter | solution.py:270
  375.5 1.6 copy-start.12
  375.6 1.6 copy-start.20
  375.6 1.6 copy-start.22
  375.6 135.9 %reduce-scatter.13.cloned.1.call-start = ((), (), s32[]{:S(2)}) async-start(), calls=%async_computation.15 | async-start | bytes 1474560 | tf_op jit(solution)/shard_map/reduce_scatter | solution.py:295
  377.1 220.5 %reduce-scatter.15.cloned.1.call-start = ((), (), s32[]{:S(2)}) async-start(), calls=%async_computation.16 | async-start | bytes 5898240 | tf_op jit(solution)/shard_map/reduce_scatter | solution.py:313
  380.8 1.4 copy-start.8
  380.8 304.9 %reduce-scatter.17.cloned.1.call-start = ((), (), s32[]{:S(2)}) async-start(), calls=%async_computation.17 | async-start | bytes 5898240 | tf_op jit(solution)/shard_map/reduce_scatter | solution.py:319
  386.1 368.8 %reduce-scatter.11.cloned.1.call-start = ((), (), s32[]{:S(2)}) async-start(), calls=%async_computation.14 | async-start | bytes 4423680 | tf_op jit(solution)/shard_map/reduce_scatter | solution.py:286
  484.5 348.9 %all-reduce.23.cloned.1.call-start = ((), (), s32[]{:S(2)}) async-start(), calls=%async_computation.18 | async-start | bytes 7077888 | tf_op jit(solution)/shard_map/psum | solution.py:327
  754.9 1.4 copy-start.35
  754.9 1.8 copy-start.24
  754.9 1.8 copy-start.31
  756.7 4.1 copy-start.25
  756.7 4.1 copy-start.26
  756.7 4.1 copy-start.27
  756.7 4.1 copy-start.32
  833.4 2.6 copy-start.18
  833.4 3.5 copy-start.15
  836.8 1.7 copy-start.14
  (1 other events, 0.7 us)
Sparse Core Ops, SparseCore 0:
  9.6 72.8 all-gather.7
  86.3 24.5 all-gather.9
  113.4 25.8 all-gather.11
  140.7 30.4 all-gather.13
  172.6 88.5 all-gather.15
  262.6 87.8 all-gather.17
  374.9 54.4 reduce-scatter.6
  433.1 46.2 reduce-scatter.8
  482.3 29.1 reduce-scatter.12
  513.7 83.9 reduce-scatter.14
  600.0 85.7 reduce-scatter.16
  687.9 66.8 reduce-scatter.10
  758.6 74.7 all-reduce.22
where the time goes:
time: 847 us
  waiting for transfers between devices  666 us (79%)
  blocking collectives  64.5 us (8%)
  matrix products  51.2 us (6%)
  local copies, waits for them, and re-layouts  24.2 us (3%)
  other arithmetic  23.9 us (3%)
  between operations  16.3 us (2%)
    reduce_scatter x1, waiting for transfers between devices, shards(): lax.psum_scatter(grad_down.astype(jnp.bfloat16), 'fsdp', scatter_dimensio...  88.1 us
    all_gather x1, waiting for transfers between devices, shards(): lax.all_gather(up_weight, 'fsdp', axis=0, tiled=True)  87.4 us
    reduce_scatter x1, waiting for transfers between devices, shards(): lax.psum_scatter(grad_up.astype(jnp.bfloat16), 'fsdp', scatter_dimension=...  86.1 us
    all_gather x1, waiting for transfers between devices, shards(): lax.all_gather(down_weight, 'fsdp', axis=0, tiled=True)  86.1 us
    reduce_scatter x1, waiting for transfers between devices, shards(): lax.psum_scatter(grad_qkv.astype(jnp.bfloat16), 'fsdp', scatter_dimension...  69.1 us
    reduce_scatter x1, waiting for transfers between devices, shards(): lax.psum_scatter(value_terms, 'ctx', scatter_dimension=1, tiled=True)  49 us
    all_gather x1, waiting for transfers between devices, shards(): lax.all_gather(qkv_weight, 'fsdp', axis=0, tiled=True)  43.2 us
    reduce_scatter x1, waiting for transfers between devices, shards(): lax.psum_scatter(key_terms, 'ctx', scatter_dimension=1, tiled=True)  43 us
  transfers between devices with their start and end apart: 13, of which 13 were waited for; matrix products, arithmetic and copies ran while one was open for 7% of the time, Pallas kernels for 0%

commit v1 on v0

v1 whole, which is shorter than its diff:
```python
import functools
import math

import jax
import jax.numpy as jnp
from jax import lax
from jax.experimental import pallas as pl
from jax.experimental.pallas import tpu as pltpu
from jax.sharding import PartitionSpec as P

HD = 64
EPS = 1e-05
NEG = -1e30
GELU_C = 0.7978845608028654
GELU_A = 0.044715
MESH = pl.DeviceIdType.MESH
BF = jnp.bfloat16
F32 = jnp.float32


def gelu_pair(values):
    inner = GELU_C * (values + GELU_A * values * values * values)
    tanh_val = jnp.tanh(inner)
    result = 0.5 * values * (1.0 + tanh_val)
    slope = 0.5 * (1.0 + tanh_val) + 0.5 * values * (1.0 - tanh_val * tanh_val) * GELU_C * (
        1.0 + 3.0 * GELU_A * values * values
    )
    return (result, slope)


def norm_rows(values, gain, shift):
    mean = jnp.mean(values, axis=-1, keepdims=True)
    centred = values - mean
    inv_std = lax.rsqrt(jnp.mean(centred * centred, axis=-1, keepdims=True) + EPS)
    normed = centred * inv_std
    return (normed * gain + shift, normed, inv_std)


def norm_back(grad_out, normed, inv_std, gain):
    scaled = grad_out * gain
    return inv_std * (
        scaled
        - jnp.mean(scaled, axis=-1, keepdims=True)
        - normed * jnp.mean(scaled * normed, axis=-1, keepdims=True)
    )


def matmul(left, right):
    return jnp.dot(left, right, preferred_element_type=F32)


def inner_rows(left, right):
    return lax.dot_general(left, right, (((0,), (0,)), ((), ())), preferred_element_type=F32)


def outer_cols(left, right):
    return lax.dot_general(left, right, (((1,), (1,)), ((), ())), preferred_element_type=F32)


def greet(devices):
    barrier = pltpu.get_barrier_semaphore()
    for device in devices:
        pl.semaphore_signal(barrier, inc=1, device_id=device, device_id_type=MESH)
    pl.semaphore_wait(barrier, len(devices))


def push(src, dst, send_sem, recv_sem, device):
    return pltpu.make_async_remote_copy(
        src_ref=src, dst_ref=dst, send_sem=send_sem, recv_sem=recv_sem,
        device_id=device, device_id_type=MESH,
    )


def gather_kernel(n, m, a_count, z_count, *refs):
    ins = refs[: a_count + z_count]
    outs = refs[a_count + z_count : 2 * (a_count + z_count)]
    a_send, a_recv, a_fwd, z_send, z_recv, local = refs[2 * (a_count + z_count) :]
    me, zed = lax.axis_index("ctx"), lax.axis_index("fsdp")
    core, chip = lax.rem(me, 2), lax.div(me, 2)
    chips = n // 2
    sib = me + 1 - 2 * core
    peers = [2 * lax.rem(chip + k, chips) + core for k in range(1, chips)]
    sources = [2 * lax.rem(chip + chips - k, chips) + core for k in range(1, chips)]
    zeds = [lax.rem(zed + k, m) for k in range(1, m)]
    devices = []
    if a_count:
        devices += [(sib, zed)] + [(p, zed) for p in peers]
    if z_count:
        devices += [(me, z) for z in zeds]
    greet(devices)
    sends = []
    locals_ = []
    for a in range(a_count):
        for k, p in enumerate(peers):
            sends.append(push(ins[a], outs[a].at[me], a_send.at[a, k], a_recv.at[a, me], (p, zed)))
            sends[-1].start()
        sends.append(
            push(ins[a], outs[a].at[me], a_send.at[a, chips - 1], a_recv.at[a, me], (sib, zed))
        )
        sends[-1].start()
    for i in range(z_count):
        b = a_count + i
        for k, z in enumerate(zeds):
            sends.append(push(ins[b], outs[b].at[zed], z_send.at[i, k], z_recv.at[i, zed], (me, z)))
            sends[-1].start()
    for b in range(a_count + z_count):
        slot = me if b < a_count else zed
        locals_.append(pltpu.make_async_copy(ins[b], outs[b].at[slot], local.at[b]))
        locals_[-1].start()
    for a in range(a_count):
        for k, s in enumerate(sources):
            push(ins[a], outs[a].at[s], a_fwd.at[a, k], a_recv.at[a, s], (sib, zed)).wait_recv()
            sends.append(
                push(outs[a].at[s], outs[a].at[s], a_fwd.at[a, k], a_recv.at[a, s], (sib, zed))
            )
            sends[-1].start()
    for a in range(a_count):
        for s in [sib] + [s + 1 - 2 * core for s in sources]:
            push(ins[a], outs[a].at[s], a_send.at[a, 0], a_recv.at[a, s], (sib, zed)).wait_recv()
    for i in range(z_count):
        b = a_count + i
        for z in zeds:
            push(ins[b], outs[b].at[z], z_send.at[i, 0], z_recv.at[i, z], (me, z)).wait_recv()
    for copy in locals_:
        copy.wait()
    for copy in sends:
        copy.wait_send()


def gather(n, m, over_ctx, over_fsdp, ident):
    arrays = tuple(over_ctx) + tuple(over_fsdp)
    a, z = len(over_ctx), len(over_fsdp)
    out_shape = [jax.ShapeDtypeStruct((n,) + v.shape, v.dtype) for v in over_ctx]
    out_shape += [jax.ShapeDtypeStruct((m,) + v.shape, v.dtype) for v in over_fsdp]
    dma = pltpu.SemaphoreType.DMA
    return pl.pallas_call(
        functools.partial(gather_kernel, n, m, a, z),
        out_shape=out_shape,
        in_specs=[pl.BlockSpec(memory_space=pl.ANY)] * (a + z),
        out_specs=[pl.BlockSpec(memory_space=pl.ANY)] * (a + z),
        scratch_shapes=[
            dma((max(a, 1), n // 2)),
            dma((max(a, 1), n)),
            dma((max(a, 1), n // 2)),
            dma((max(z, 1), m)),
            dma((max(z, 1), m)),
            dma((a + z,)),
        ],
        compiler_params=pltpu.CompilerParams(collective_id=ident, has_side_effects=True),
    )(*arrays)


def scatter_kernel(n, x_ref, o_ref, one, pair, two, s1, r1, s2, r2):
    me, zed = lax.axis_index("ctx"), lax.axis_index("fsdp")
    core, chip = lax.rem(me, 2), lax.div(me, 2)
    chips = n // 2
    sib = me + 1 - 2 * core
    order = [lax.rem(chip + k, chips) for k in range(1, chips)] + [chip]
    greet([(sib, zed)] + [(2 * j + core, zed) for j in order[:-1]])
    first = []
    for k, j in enumerate(order):
        first.append(push(x_ref.at[2 * j + 1 - core], one.at[k], s1.at[k], r1.at[k], (sib, zed)))
        first[-1].start()
    second = []
    for k, j in enumerate(order):
        first[k].wait_recv()
        total = x_ref[2 * j + core].astype(F32) + one[k].astype(F32)
        if k < chips - 1:
            pair[k] = total.astype(BF)
            second.append(
                push(pair.at[k], two.at[k], s2.at[k], r2.at[k], (2 * j + core, zed))
            )
            second[-1].start()
        else:
            o_ref[...] = total
    for k in range(chips - 1):
        second[k].wait_recv()
        o_ref[...] += two[k].astype(F32)
    for copy in first + second:
        copy.wait_send()


def scatter(n, x, ident):
    _, rows, cols = x.shape
    chips = n // 2
    dma = pltpu.SemaphoreType.DMA
    return pl.pallas_call(
        functools.partial(scatter_kernel, n),
        out_shape=jax.ShapeDtypeStruct((rows, cols), F32),
        in_specs=[pl.BlockSpec(memory_space=pltpu.VMEM)],
        out_specs=pl.BlockSpec(memory_space=pltpu.VMEM),
        scratch_shapes=[
            pltpu.VMEM((chips, rows, cols), BF),
            pltpu.VMEM((chips - 1, rows, cols), BF),
            pltpu.VMEM((chips - 1, rows, cols), BF),
            dma((chips,)),
            dma((chips,)),
            dma((chips - 1,)),
            dma((chips - 1,)),
        ],
        compiler_params=pltpu.CompilerParams(
            collective_id=ident, has_side_effects=True, vmem_limit_bytes=48 << 20
        ),
    )(x)


def swap_kernel(n, x_ref, o_ref, send, recv, local):
    me, zed = lax.axis_index("ctx"), lax.axis_index("fsdp")
    others = [lax.rem(me + k, n) for k in range(1, n)]
    greet([(j, zed) for j in others])
    sends = []
    for k, j in enumerate(others):
        sends.append(push(x_ref.at[j], o_ref.at[me], send.at[k], recv.at[me], (j, zed)))
        sends[-1].start()
    own = pltpu.make_async_copy(x_ref.at[me], o_ref.at[me], local)
    own.start()
    own.wait()
    for k, j in enumerate(others):
        push(x_ref.at[j], o_ref.at[j], send.at[k], recv.at[j], (j, zed)).wait_recv()
    for copy in sends:
        copy.wait_send()


def swap(n, x, ident):
    dma = pltpu.SemaphoreType.DMA
    return pl.pallas_call(
        functools.partial(swap_kernel, n),
        out_shape=jax.ShapeDtypeStruct(x.shape, x.dtype),
        in_specs=[pl.BlockSpec(memory_space=pltpu.VMEM)],
        out_specs=pl.BlockSpec(memory_space=pltpu.VMEM),
        scratch_shapes=[dma((n,)), dma((n,)), dma],
        compiler_params=pltpu.CompilerParams(collective_id=ident, has_side_effects=True),
    )(x)


def shards(
    n,
    m,
    layer_input,
    qkv_weight,
    query_bias,
    value_bias,
    out_weight,
    out_bias,
    first_gain,
    first_shift,
    second_gain,
    second_shift,
    up_weight,
    up_bias,
    down_weight,
    down_bias,
    out_grad,
):
    seqs, block, width = layer_input.shape
    rows = seqs * block
    length = n * block
    heads = width // HD
    scale = 1.0 / math.sqrt(HD)
    me, zed = lax.axis_index("ctx"), lax.axis_index("fsdp")
    hp = -(-heads // n)
    while heads % hp:
        hp += 1
    active_n = heads // hp
    hw = hp * HD
    valid = me < active_n
    head_at = jnp.minimum(me, active_n - 1)
    share = width // m
    hidden_share = up_bias.shape[0]
    fpart = hidden_share // n
    ff = hidden_share * m
    fown = m * fpart

    x_local = layer_input.reshape(rows, width)
    g_local = out_grad.reshape(rows, width)
    qkv_own = lax.dynamic_index_in_dim(
        qkv_weight.reshape(share, 3, active_n, hw), head_at, 2, keepdims=False
    ).reshape(share, 3 * hw)
    up_own = lax.dynamic_index_in_dim(
        up_weight.reshape(share, m, n, fpart), me, 2, keepdims=False
    ).reshape(share, fown)
    down_own = lax.dynamic_index_in_dim(
        down_weight.reshape(n, fpart, width), me, 0, keepdims=False
    )
    out_own = lax.dynamic_index_in_dim(
        out_weight.reshape(n, share // n, width), me, 0, keepdims=False
    )
    vectors = jnp.concatenate(
        [query_bias, value_bias, out_bias, first_gain, first_shift, second_gain, second_shift,
         down_bias, up_bias]
    ).astype(F32)
    span = vectors.shape[0]
    padded = -(-span // 1024) * 1024
    vectors = jnp.pad(vectors, (0, padded - span)).reshape(padded // 128, 128)

    x_all, qkv_all, vec_all = gather(n, m, [x_local], [qkv_own, vectors], 0)
    up_mat = lax.all_gather(up_own, "fsdp", axis=0, tiled=True)
    down_mat = lax.all_gather(down_own, "fsdp", axis=0, tiled=True)
    out_mat = lax.all_gather(out_own, ("fsdp", "ctx"), axis=0, tiled=True)
    g_all = lax.all_gather(g_local, "ctx", axis=0, tiled=True)

    qkv_mat = jnp.where(valid, qkv_all.reshape(width, 3 * hw), jnp.zeros((), BF))
    vec_all = vec_all.reshape(m, padded)
    pieces = [vec_all[:, i * share : (i + 1) * share].reshape(width) for i in range(8)]
    q_bias, v_bias, out_shift, gain_one, shift_one, gain_two, shift_two, down_shift = pieces
    up_shift = lax.dynamic_index_in_dim(
        vec_all[:, 8 * share : span].reshape(m, n, fpart), me, 1, keepdims=False
    ).reshape(fown)
    q_own = lax.dynamic_index_in_dim(q_bias.reshape(active_n, hw), head_at, 0, keepdims=False)
    v_own = lax.dynamic_index_in_dim(v_bias.reshape(active_n, hw), head_at, 0, keepdims=False)

    def to_seq(v):
        return (
            v.reshape(n, seqs, block, hp, HD)
            .transpose(1, 3, 0, 2, 4)
            .reshape(seqs, hp, length, HD)
        )

    def from_seq(v):
        return (
            v.reshape(seqs, hp, n, block, HD)
            .transpose(2, 0, 3, 1, 4)
            .reshape(n * rows, hw)
        )

    x_rows = x_all.reshape(n * rows, width).astype(F32)
    normed_all, _, _ = norm_rows(x_rows, gain_one, shift_one)
    mixed_in = normed_all.astype(BF)
    projected = matmul(mixed_in, qkv_mat)
    queries = to_seq((projected[:, :hw] + q_own).astype(BF))
    keys = to_seq(projected[:, hw : 2 * hw].astype(BF))
    values = to_seq((projected[:, 2 * hw :] + v_own).astype(BF))

    at = jnp.arange(length, dtype=jnp.int32)
    causal = (at[None, :] <= at[:, None])[None, None]
    scores = jnp.einsum("shqd,shkd->shqk", queries, keys, preferred_element_type=F32) * scale
    masked = jnp.where(causal, scores, NEG)
    top = jnp.max(masked, axis=-1)
    total = jnp.sum(jnp.exp(masked - top[..., None]), axis=-1)
    logsum = top + jnp.log(total)
    probs = jnp.where(causal, jnp.exp(scores - logsum[..., None]), 0.0)
    probs_b = probs.astype(BF)
    mixed = jnp.einsum("shqk,shkd->shqd", probs_b, values, preferred_element_type=F32).astype(BF)

    got = swap(n, from_seq(mixed).reshape(n, rows, hw), 1)
    attended = got[:active_n].transpose(1, 0, 2).reshape(rows, width)
    inputs = x_local.astype(F32)
    _, unit_one, inv_one = norm_rows(inputs, gain_one, shift_one)
    hidden = inputs + matmul(attended, out_mat) + out_shift
    normed_two, unit_two, inv_two = norm_rows(hidden, gain_two, shift_two)
    (ffn_in,) = gather(n, m, [normed_two.astype(BF)], [], 2)
    ffn_in = ffn_in.reshape(n * rows, width)
    lifted = matmul(ffn_in, up_mat) + up_shift
    gelu_val, gelu_slope = gelu_pair(lifted)
    active = gelu_val.astype(BF)

    grad_lifted = outer_cols(g_all, down_mat) * gelu_slope
    lifted_b = grad_lifted.astype(BF)
    part_two = outer_cols(lifted_b, up_mat).astype(BF).reshape(n, rows, width)
    grad_normed_two = scatter(n, part_two, 3)

    down_part = matmul(active, down_mat).astype(BF)
    result = hidden + down_shift + lax.psum_scatter(
        down_part, "ctx", scatter_dimension=0, tiled=True
    ).astype(F32)
    layer_output = result.astype(BF).reshape(seqs, block, width)
    grad_up_shift = jnp.sum(grad_lifted, axis=0)
    grad_down = inner_rows(active, g_all).astype(BF)
    grad_up = inner_rows(ffn_in, lifted_b).astype(BF)
    grad_down = lax.psum_scatter(grad_down, "fsdp", scatter_dimension=0, tiled=True)
    grad_up = lax.psum_scatter(grad_up, "fsdp", scatter_dimension=0, tiled=True)
    grad_down = lax.all_gather(grad_down, "ctx", axis=0, tiled=True).astype(F32)
    grad_up = (
        lax.all_gather(grad_up, "ctx", axis=0)
        .reshape(n, share, m, fpart)
        .transpose(1, 2, 0, 3)
        .reshape(share, ff)
        .astype(F32)
    )

    upstream_f = g_local.astype(F32)
    grad_gain_two = jnp.sum(grad_normed_two * unit_two, axis=0)
    grad_shift_two = jnp.sum(grad_normed_two, axis=0)
    grad_hidden = upstream_f + norm_back(grad_normed_two, unit_two, inv_two, gain_two)
    hidden_b = grad_hidden.astype(BF)
    grad_out_shift = jnp.sum(grad_hidden, axis=0)
    grad_attended = outer_cols(hidden_b, out_mat).astype(BF)
    blocks = grad_attended.reshape(rows, active_n, hw).transpose(1, 0, 2)
    blocks = jnp.pad(blocks, ((0, n - active_n), (0, 0), (0, 0)))
    grad_heads = to_seq(swap(n, blocks, 4).reshape(n * rows, hw))

    grad_out = inner_rows(attended, hidden_b).astype(BF)
    grad_out = lax.psum_scatter(grad_out, ("fsdp", "ctx"), scatter_dimension=0, tiled=True)
    grad_out = lax.all_gather(grad_out, "ctx", axis=0, tiled=True).astype(F32)

    delta = jnp.sum(grad_heads.astype(F32) * mixed.astype(F32), axis=-1)
    grad_probs = jnp.einsum("shqd,shkd->shqk", grad_heads, values, preferred_element_type=F32)
    grad_scores = (probs * (grad_probs - delta[..., None])).astype(BF)
    grad_values = jnp.einsum("shqk,shqd->shkd", probs_b, grad_heads, preferred_element_type=F32)
    grad_queries = (
        jnp.einsum("shqk,shkd->shqd", grad_scores, keys, preferred_element_type=F32) * scale
    )
    grad_keys = (
        jnp.einsum("shqk,shqd->shkd", grad_scores, queries, preferred_element_type=F32) * scale
    )
    grad_query_shift = jnp.sum(grad_queries, axis=(0, 2)).reshape(hw)
    grad_value_shift = jnp.sum(grad_values, axis=(0, 2)).reshape(hw)
    proj_b = jnp.concatenate(
        [from_seq(g.astype(BF)) for g in (grad_queries, grad_keys, grad_values)], axis=1
    )
    part_one = outer_cols(proj_b, qkv_mat).astype(BF).reshape(n, rows, width)
    grad_qkv = inner_rows(mixed_in, proj_b).astype(BF)
    grad_qkv = lax.psum_scatter(grad_qkv, "fsdp", scatter_dimension=0, tiled=True)
    grad_normed_one = scatter(n, part_one, 5)
    grad_qkv = (
        lax.all_gather(grad_qkv, "ctx", axis=0)[:active_n]
        .reshape(active_n, share, 3, hw)
        .transpose(1, 2, 0, 3)
        .reshape(share, 3 * width)
        .astype(F32)
    )
    grad_gain_one = jnp.sum(grad_normed_one * unit_one, axis=0)
    grad_shift_one = jnp.sum(grad_normed_one, axis=0)
    input_grad = (grad_hidden + norm_back(grad_normed_one, unit_one, inv_one, gain_one)).reshape(
        seqs, block, width
    )

    def place_heads(v):
        spot = (jnp.arange(active_n, dtype=jnp.int32) == me)[:, None]
        return jnp.where(spot, v[None, :], 0.0).reshape(width)

    spot = (jnp.arange(n, dtype=jnp.int32) == me)[None, :, None]
    up_placed = jnp.where(spot, grad_up_shift.reshape(m, 1, fpart), 0.0).reshape(ff)
    small = jnp.concatenate(
        [
            place_heads(grad_query_shift), place_heads(grad_value_shift), grad_out_shift,
            grad_gain_one, grad_shift_one, grad_gain_two, grad_shift_two,
            jnp.sum(upstream_f, axis=0), up_placed,
        ]
    )
    small = lax.psum(small, ("fsdp", "ctx"))
    mine = lax.dynamic_index_in_dim(
        small[: 8 * width].reshape(8, m, share), zed, 1, keepdims=False
    )
    up_mine = lax.dynamic_index_in_dim(
        small[8 * width :].reshape(m, hidden_share), zed, 0, keepdims=False
    )
    return (
        layer_output,
        input_grad,
        grad_qkv,
        mine[0],
        mine[1],
        grad_out,
        mine[2],
        mine[3],
        mine[4],
        mine[5],
        mine[6],
        grad_up,
        up_mine,
        grad_down,
        mine[7],
    )


def solution(mesh):
    vec, mat, act = P("fsdp"), P("fsdp", None), P("fsdp", "ctx", None)
    n, m = mesh.shape["ctx"], mesh.shape["fsdp"]
    return jax.shard_map(
        functools.partial(shards, n, m),
        mesh=mesh,
        in_specs=(act, mat, vec, vec, mat, vec, vec, vec, vec, vec, mat, vec, mat, vec, act),
        out_specs=(act, act, mat, vec, vec, mat, vec, vec, vec, vec, vec, mat, vec, mat, vec),
        check_vma=False,
    )
```

time: 847 us -> 465 us (0.55)
  waiting for transfers between devices: 666 us -> 142 us
  Pallas kernels: 0 us -> 83.4 us
  local copies, waits for them, and re-layouts: 24.2 us -> 68.9 us
  blocking collectives: 64.5 us -> 81.9 us
  matrix products: 51.2 us -> 42.7 us
    all_gather x6 -> x5, waiting for transfers between devices: 270 us -> 14.5 us  [the longest x1 14.5 us: shards(): lax.all_gather(grad_qkv, 'ctx', axis=0)[:active_n]]
    reduce_scatter x6 -> x5, waiting for transfers between devices: 362 us -> 126 us  [the longest x1 83.6 us: shards(): lax.psum_scatter(grad_out, ('fsdp', 'ctx'), scatter_dimension=0, tiled=True)]
    pallas_call x0 -> x6, Pallas kernels: none -> 83.4 us  [the longest x2 35.2 us: gather(): pl.pallas_call(functools.partial(gather_kernel, n, m, a, z), out_shape=ou...]
    unnamed x2 -> x0, blocking collectives: 39.2 us -> none
    psum x1 -> x0, waiting for transfers between devices: 30.5 us -> none  [shards(): lax.psum(owned[0].astype(jnp.bfloat16), 'ctx').astype(jnp.float32)]
    all_gather x1 -> x3, blocking collectives: 13 us -> 43.5 us  [the longest x1 17 us: shards(): up_mat = lax.all_gather(up_own, 'fsdp', axis=0, tiled=True)]
    psum x1, blocking collectives: 12.2 us -> 38.4 us  [shards(): small = lax.psum(small, ('fsdp', 'ctx'))]
    convert_element_type x5 -> x9, local copies, waits for them, and re-layouts: 1.3 us -> 21.3 us  [the longest x3 11.3 us: shards(): grad_up = lax.all_gather(grad_up, 'ctx', axis=0).reshape(n, share, m, fpa...]
  transfers between devices with their start and end apart: 13 -> 10, of which waited for: 13 -> 5; matrix products, arithmetic and copies ran while one was open for 7% -> 25% of each run, Pallas kernels for 0% -> 18%
where the time goes in v1:
time: 465 us; the launch traced here: 457 us
  waiting for transfers between devices  142 us (31%)
  Pallas kernels  83.4 us (18%)
  blocking collectives  81.9 us (18%)
  local copies, waits for them, and re-layouts  68.9 us (15%)
  matrix products  42.7 us (9%)
  other arithmetic  22.1 us (5%)
  between operations  15.5 us (3%)
    reduce_scatter x1, waiting for transfers between devices, shards(): lax.psum_scatter(grad_out, ('fsdp', 'ctx'), scatter_dimension=0, tiled=True)  83.6 us
    psum x1, blocking collectives, shards(): small = lax.psum(small, ('fsdp', 'ctx'))  38.4 us
    pallas_call x2, Pallas kernels, gather(): pl.pallas_call(functools.partial(gather_kernel, n, m, a, z), out_shape=ou...  35.2 us
    pallas_call x2, Pallas kernels, scatter(): pl.pallas_call(functools.partial(scatter_kernel, n), out_shape=jax.ShapeD...  32.5 us
    reduce_scatter x1, waiting for transfers between devices, shards(): lax.psum_scatter(grad_qkv, 'fsdp', scatter_dimension=0, tiled=True)  18.4 us
    all_gather x1, blocking collectives, shards(): up_mat = lax.all_gather(up_own, 'fsdp', axis=0, tiled=True)  17 us
    all_gather x1, blocking collectives, shards(): down_mat = lax.all_gather(down_own, 'fsdp', axis=0, tiled=True)  16.9 us
    reduce_scatter x1, waiting for transfers between devices, shards(): lax.psum_scatter(grad_down, 'fsdp', scatter_dimension=0, tiled=True)  16.2 us
  transfers between devices with their start and end apart: 10, of which 5 were waited for; matrix products, arithmetic and copies ran while one was open for 25% of the time, Pallas kernels for 18%

profile of v1, /device:TPU:0, one launch (start us, length us, event | category | flops | bytes accessed | tf_op | source)
XLA Modules:
  0.0 457.4 jit_solution(8839730829977020943)
XLA Ops:
  11.0 6.1 %concatenate.9 = bf16[2304]{0:T(1024)(128)(2,1)S(1)} concatenate(bf16[192]{0:T(256)(128)(2,1)} %param.17, bf16[192]{0:T(256)(128)(2,1)} %param.18, bf16[192]{0:T(256)(128)(2,1)} %param.20, bf16[192]{0:T(256)(128)(2,1)} %param.21, bf16[192]{0:T(256)(128)(2,1)} %param.22, bf16[192]{0:T(256)(128)(2,1)} %param.23, bf16[192]{0:T(256)(128)(2,1)} %param.24, bf16[192]{0:T(256)(128)(2,1)} %param.28, ...), dimensions={0} | concatenate | bytes 9216 | tf_op jit(solution)/shard_map/concatenate | solution.py:288
  20.3 21.8 %shard_map.262 = (bf16[8,128,768]{2,1,0:T(8,128)(2,1)}, bf16[4,192,384]{2,1,0:T(8,128)(2,1)}, f32[4,24,128]{2,1,0:T(8,128)}) custom-call(bf16[128,768]{1,0:T(8,128)(2,1)} %bitcast.223, bf16[192,384]{1,0:T(8,128)(2,1)} %bitcast.245, f32[24,128]{1,0:T(8,128)} %bitcast_convert_fusion.refs_2_), custom_call_target="tpu_custom_call" | custom-call | tf_op jit(solution)/shard_map/pallas_call | solution.py:136
  43.1 1.8 convert_reduce_fusion
  53.2 1.7 copy.75
  55.9 1.8 copy.46
  57.7 1.7 copy.73
  59.4 1.8 reshape.421
  61.2 3.2 select_reduce_fusion
  64.4 2.2 exponential_reduce_fusion
  68.2 2.2 convolution_convert_fusion.6
  71.2 3.9 reshape.426
  75.0 2.8 dynamic-slice_reduce_fusion
  82.2 1.9 copy.49.x_ref
  84.1 7.6 %shard_map.263 = bf16[8,128,128]{2,1,0:T(8,128)(2,1)} custom-call(bf16[8,128,128]{2,1,0:T(8,128)(2,1)} %copy.49.x_ref), custom_call_target="tpu_custom_call" | custom-call | tf_op jit(solution)/shard_map/pallas_call | solution.py:226
  94.4 16.9 %all-gather.1 = bf16[1,384,768]{2,1,0:T(8,128)(2,1)} all-gather(bf16[1,96,768]{2,1,0:T(8,128)(2,1)S(1)} %constant_dynamic-slice_fusion.9), channel_id=3, replica_groups=mesh['ctx'=8,'fsdp'=4] {'fsdp'}, dimensions={1}, use_global_device_ids=true | all-gather | bytes 737280 | tf_op jit(solution)/shard_map/all_gather | solution.py:298
  111.3 17.0 %all_gather.31 = bf16[768,384]{1,0:T(8,128)(2,1)} all-gather(bf16[192,384]{1,0:T(8,128)(2,1)S(1)} %copy-done.20), channel_id=1, replica_groups=mesh['ctx'=8,'fsdp'=4] {'fsdp'}, dimensions={0}, use_global_device_ids=true | all-gather | bytes 737280 | tf_op jit(solution)/shard_map/all_gather | solution.py:297
  128.4 1.7 fusion.64
  131.1 13.4 %shard_map.264 = bf16[8,128,768]{2,1,0:T(8,128)(2,1)} custom-call(bf16[128,768]{1,0:T(8,128)(2,1)} %add_convert_fusion.2.refs_0_), custom_call_target="tpu_custom_call" | custom-call | tf_op jit(solution)/shard_map/pallas_call | solution.py:136
  144.6 2.6 convolution_add_fusion
  148.3 2.4 convolution_convert_fusion.2
  151.5 1.8 fusion.4
  153.2 4.0 fusion.65
  158.1 1.8 convolution_convert_fusion.4
  160.0 2.5 convolution_convert_fusion.1
  162.5 18.0 %shard_map.265 = f32[128,768]{1,0:T(8,128)S(1)} custom-call(bf16[8,128,768]{2,1,0:T(8,128)(2,1)S(1)} %bitcast.220), custom_call_target="tpu_custom_call" | custom-call | tf_op jit(solution)/shard_map/pallas_call | solution.py:187
  180.8 1.8 fusion.17
  182.9 8.1 %reduce-scatter.6.cloned.1.call-done = bf16[128,768]{1,0:T(8,128)(2,1)} async-done(((bf16[1024,768]{1,0:T(8,128)(2,1)}), bf16[128,768]{1,0:T(8,128)(2,1)}) %reduce-scatter.6.cloned.1.call-update) | async-done | bytes 196624 | tf_op jit(solution)/shard_map/reduce_scatter | solution.py:363
  191.0 1.8 fusion.59
  194.4 8.2 %shard_map.266 = bf16[8,128,128]{2,1,0:T(8,128)(2,1)} custom-call(bf16[8,128,128]{2,1,0:T(8,128)(2,1)} %pad.10.x_ref), custom_call_target="tpu_custom_call" | custom-call | tf_op jit(solution)/shard_map/pallas_call | solution.py:226
  204.2 5.8 %fusion.61 = (f32[2,64]{1,0:T(2,128)S(1)}, bf16[2,1024,64]{1,2,0:T(8,128)(2,1)S(1)}) fusion(bf16[2,1024,64]{1,2,0:T(8,128)(2,1)S(1)} %reshape.434, f32[2,1024,1024]{1,2,0:T(8,128)} %copy-done.3, f32[2,1024]{1,0:T(2,128)S(1)} %copy-done.36, pred[1024,1024]{0,1:T(8,128)(4,1)S(1)} %copy-done.7), kind=kOutput, calls=%fused_computation.139 | convolution fusion | flops 277086080 | bytes 9970176 | tf_op jit(solution)/shard_map/shqk,shqd->shkd/dot_general | solution.py:399
  209.9 5.3 %multiply_convert_fusion = bf16[2,1024,1024]{1,2,0:T(8,128)(2,1)S(1)} fusion(f32[2,1024,1024]{1,2,0:T(8,128)} %copy-done.3, f32[2,1024]{1,0:T(2,128)S(1)} %multiply_reduce_fusion.1, f32[2,1024]{1,0:T(2,128)S(1)} %copy-done.36, pred[1024,1024]{0,1:T(8,128)(4,1)S(1)} %copy-done.7, bf16[2,1024,64]{1,2,0:T(8,128)(2,1)S(1)} %reshape.434, ...), kind=kOutput, calls=%fused_computation | convolution fusion | flops 281018368 | bytes 14172160 | tf_op jit(solution)/shard_map/shqd,shkd->shqk/dot_general | solution.py:397
  219.3 1.8 convolution_convert_fusion.5
  222.0 16.2 %reduce-scatter.14.cloned.1.call-done = bf16[96,768]{1,0:T(8,128)(2,1)} async-done(((bf16[384,768]{1,0:T(8,128)(2,1)}), bf16[96,768]{1,0:T(8,128)(2,1)}) %reduce-scatter.14.cloned.1.call-update) | async-done | bytes 147472 | tf_op jit(solution)/shard_map/reduce_scatter | solution.py:370
  240.5 2.3 convolution_convert_fusion
  242.9 18.4 %reduce-scatter.8.cloned.1.call-done = bf16[192,384]{1,0:T(8,128)(2,1)} async-done(((bf16[768,384]{1,0:T(8,128)(2,1)}), bf16[192,384]{1,0:T(8,128)(2,1)}) %reduce-scatter.8.cloned.1.call-update) | async-done | bytes 147472 | tf_op jit(solution)/shard_map/reduce_scatter | solution.py:413
  261.5 14.5 %shard_map.267 = f32[128,768]{1,0:T(8,128)S(1)} custom-call(bf16[8,128,768]{2,1,0:T(8,128)(2,1)S(1)} %bitcast.219), custom_call_target="tpu_custom_call" | custom-call | tf_op jit(solution)/shard_map/pallas_call | solution.py:187
  276.4 38.4 %psum.7 = f32[9216]{0:T(1024)S(1)} all-reduce(f32[9216]{0:T(1024)S(1)} %constant_dynamic-update-slice_fusion.1), channel_id=1, replica_groups=mesh['ctx'=8,'fsdp'=4] {'fsdp','ctx'}, use_global_device_ids=true, to_apply=%region_24.25 | all-reduce | flops 9216 | bytes 73728 | tf_op jit(solution)/shard_map/psum | solution.py:441
  317.1 3.3 reshape.450
  320.4 3.5 copy.62
  323.9 4.5 reshape.448
  328.4 2.9 convert_element_type.182
  331.2 83.6 %reduce-scatter.10.cloned.1.call-done = bf16[24,768]{1,0:T(8,128)(2,1)} async-done(((bf16[768,768]{1,0:T(8,128)(2,1)}), bf16[24,768]{1,0:T(8,128)(2,1)}) %reduce-scatter.10.cloned.1.call-update) | async-done | bytes 36880 | tf_op jit(solution)/shard_map/reduce_scatter | solution.py:393
  414.9 9.5 %all_gather.36 = bf16[192,768]{1,0:T(8,128)(2,1)S(1)} all-gather(bf16[24,768]{1,0:T(8,128)(2,1)} %reduce-scatter.10.cloned.1.call-done), channel_id=1, replica_groups=mesh['ctx'=8,'fsdp'=4] {'ctx'}, dimensions={0}, use_global_device_ids=true | all-gather | bytes 331776 | tf_op jit(solution)/shard_map/all_gather | solution.py:394
  425.3 14.5 %all-gather.17.cloned.1.call-done = bf16[1536,384]{1,0:T(8,128)(2,1)} async-done(((bf16[192,384]{1,0:T(8,128)(2,1)}), bf16[1536,384]{1,0:T(8,128)(2,1)}) %all-gather.17.cloned.1.call-update) | async-done | bytes 1179664 | tf_op jit(solution)/shard_map/all_gather | solution.py:416
  439.8 2.5 slice_convert_fusion
  442.2 2.7 reshape.449
  444.9 2.5 copy.61
  447.4 2.7 reshape.447
  (206 shorter events, 44.8 us)
Async XLA Ops:
  7.2 87.2 %copy-start = (bf16[768,768]{1,0:T(8,128)(2,1)S(1)}, bf16[768,768]{1,0:T(8,128)(2,1)}, u32[]{:S(2)}) copy-start(bf16[768,768]{1,0:T(8,128)(2,1)} %param.27) | copy-start | bytes 3538948
  7.2 10.5 %copy-start.16 = (bf16[192,2304]{1,0:T(8,128)(2,1)S(1)}, bf16[192,2304]{1,0:T(8,128)(2,1)}, u32[]{:S(2)}) copy-start(bf16[192,2304]{1,0:T(8,128)(2,1)} %param.16) | copy-start | bytes 2654212
  7.2 121.1 %all-gather.13.cloned.1.call-start = ((), (), s32[]{:S(2)}) async-start(), calls=%async_computation.11 | async-start | bytes 1216512 | tf_op jit(solution)/shard_map/all_gather | solution.py:299
  8.8 144.4 %all-gather.15.cloned.1.call-start = ((), (), s32[]{:S(2)}) async-start(), calls=%async_computation.12 | async-start | bytes 1769472 | tf_op jit(solution)/shard_map/all_gather | solution.py:300
  9.6 181.4 %reduce-scatter.6.cloned.1.call-start = ((), (), s32[]{:S(2)}) async-start(), calls=%async_computation.5 | async-start | bytes 1769472 | tf_op jit(solution)/shard_map/reduce_scatter | solution.py:363
  42.1 3.3 copy-start.2
  43.1 3.6 copy-start.23
  43.1 4.6 copy-start.19
  47.4 1.0 copy-start.24
  47.5 0.9 copy-start.29
  47.7 0.8 copy-start.17
  52.3 8.9 %copy-start.12 = (bf16[2,1024,64]{1,2,0:T(8,128)(2,1)}, bf16[2,1024,64]{1,2,0:T(8,128)(2,1)S(1)}, u32[]{:S(2)}) copy-start(bf16[2,1024,64]{1,2,0:T(8,128)(2,1)S(1)} %reshape.417) | copy-start | bytes 786436
  61.2 3.2 copy-start.6
  64.4 3.2 copy-start.3
  64.4 3.8 copy-start.21
  70.5 11.0 %copy-start.14 = (bf16[2,1024,64]{1,2,0:T(8,128)(2,1)}, bf16[2,1024,64]{1,2,0:T(8,128)(2,1)S(1)}, u32[]{:S(2)}) copy-start(bf16[2,1024,64]{1,2,0:T(8,128)(2,1)S(1)} %convolution_convert_fusion.6) | copy-start | bytes 786436
  82.2 29.1 %copy-start.20 = (bf16[192,384]{1,0:T(8,128)(2,1)S(1)}, bf16[192,384]{1,0:T(8,128)(2,1)}, u32[]{:S(2)}) copy-start(bf16[192,384]{1,0:T(8,128)(2,1)} %reshape.427) | copy-start | bytes 442372
  84.1 44.3 %copy-start.4 = (bf16[1,128,768]{2,1,0:T(8,128)(2,1)S(1)}, bf16[1,128,768]{2,1,0:T(8,128)(2,1)}, u32[]{:S(2)}) copy-start(bf16[1,128,768]{2,1,0:T(8,128)(2,1)} %param.15) | copy-start | bytes 589828
  111.3 19.0 %copy-start.27 = (f32[768]{0:T(1024)S(1)}, f32[768]{0:T(1024)}, u32[]{:S(2)}) copy-start(f32[768]{0:T(1024)} %mul.201) | copy-start | bytes 9220
  111.3 19.0 %copy-start.33 = (f32[768]{0:T(1024)S(1)}, f32[768]{0:T(1024)}, u32[]{:S(2)}) copy-start(f32[768]{0:T(1024)} %add.199) | copy-start | bytes 9220
  130.1 14.5 %copy-start.37 = (f32[384]{0:T(512)S(1)}, f32[384]{0:T(512)}, u32[]{:S(2)}) copy-start(f32[384]{0:T(512)} %add.202) | copy-start | bytes 4612
  144.6 3.8 copy-start.18
  147.2 1.1 copy-start.40
  150.7 0.8 copy-start.30
  150.7 0.8 copy-start.31
  150.7 70.5 %reduce-scatter.12.cloned.1.call-start = ((), (), s32[]{:S(2)}) async-start(), calls=%async_computation.8 | async-start | bytes 737280 | tf_op jit(solution)/shard_map/reduce_scatter | solution.py:371
  153.2 4.9 %copy-start.11 = (bf16[8,128,768]{2,1,0:T(8,128)(2,1)S(1)}, bf16[8,128,768]{2,1,0:T(8,128)(2,1)}, u32[]{:S(2)}) copy-start(bf16[8,128,768]{2,1,0:T(8,128)(2,1)} %shard_map.264) | copy-start | bytes 4718596
  157.2 0.9 copy-start.39
  160.0 78.2 %reduce-scatter.14.cloned.1.call-start = ((), (), s32[]{:S(2)}) async-start(), calls=%async_computation.9 | async-start | bytes 737280 | tf_op jit(solution)/shard_map/reduce_scatter | solution.py:370
  160.0 20.8 %copy-start.41 = (f32[1024,384]{1,0:T(8,128)S(1)}, f32[1024,384]{1,0:T(8,128)}, u32[]{:S(2)}) copy-start(f32[1024,384]{1,0:T(8,128)} %copy-done.40) | copy-start | bytes 4718596
  162.5 18.0 %copy-start.28 = (f32[768]{0:T(1024)S(1)}, f32[768]{0:T(1024)}, u32[]{:S(2)}) copy-start(f32[768]{0:T(1024)} %mul.201) | copy-start | bytes 9220
  162.5 18.3 %copy-start.38 = (bf16[1,1024,768]{2,1,0:T(8,128)(2,1)S(1)}, bf16[1,1024,768]{2,1,0:T(8,128)(2,1)}, u32[]{:S(2)}) copy-start(bf16[1,1024,768]{2,1,0:T(8,128)(2,1)} %all-gather.15.cloned.1.call-done) | copy-start | bytes 4718596
  180.8 10.2 %copy-start.8 = (bf16[1,128,768]{2,1,0:T(8,128)(2,1)S(1)}, bf16[1,128,768]{2,1,0:T(8,128)(2,1)}, u32[]{:S(2)}) copy-start(bf16[1,128,768]{2,1,0:T(8,128)(2,1)} %param.29) | copy-start | bytes 589828
  182.6 10.2 %copy-start.5 = (bf16[1,768,768]{2,1,0:T(8,128)(2,1)S(1)}, bf16[1,768,768]{2,1,0:T(8,128)(2,1)}, u32[]{:S(2)}) copy-start(bf16[1,768,768]{2,1,0:T(8,128)(2,1)} %all-gather.13.cloned.1.call-done) | copy-start | bytes 3538948
  182.6 78.7 %reduce-scatter.8.cloned.1.call-start = ((), (), s32[]{:S(2)}) async-start(), calls=%async_computation.6 | async-start | bytes 737280 | tf_op jit(solution)/shard_map/reduce_scatter | solution.py:413
  193.5 10.5 %copy-start.15 = (bf16[2,1024,64]{1,2,0:T(8,128)(2,1)S(1)}, bf16[2,1024,64]{1,2,0:T(8,128)(2,1)}, u32[]{:S(2)}) copy-start(bf16[2,1024,64]{1,2,0:T(8,128)(2,1)} %copy-done.14) | copy-start | bytes 786436
  193.7 10.4 %copy-start.7 = (pred[1024,1024]{0,1:T(8,128)(4,1)S(1)}, pred[1024,1024]{0,1:T(8,128)(4,1)}, u32[]{:S(2)}) copy-start(pred[1024,1024]{0,1:T(8,128)(4,1)} %iota_compare_fusion) | copy-start | bytes 3145732
  193.7 10.4 %copy-start.36 = (f32[2,1024]{1,0:T(2,128)S(1)}, f32[2,1024]{1,0:T(2,128)}, u32[]{:S(2)}) copy-start(f32[2,1024]{1,0:T(2,128)} %copy-done.35) | copy-start | bytes 24580
  204.2 5.8 %copy-start.22 = (bf16[2,1024,64]{1,2,0:T(8,128)(2,1)S(1)}, bf16[2,1024,64]{1,2,0:T(8,128)(2,1)}, u32[]{:S(2)}) copy-start(bf16[2,1024,64]{1,2,0:T(8,128)(2,1)} %reshape.421) | copy-start | bytes 786436
  209.9 5.4 %copy-start.13 = (bf16[2,1024,64]{1,2,0:T(8,128)(2,1)S(1)}, bf16[2,1024,64]{1,2,0:T(8,128)(2,1)}, u32[]{:S(2)}) copy-start(bf16[2,1024,64]{1,2,0:T(8,128)(2,1)} %copy-done.12) | copy-start | bytes 786436
  217.6 1.7 copy-start.10
  217.9 0.9 copy-start.26
  221.2 95.9 %all-gather.19.cloned.1.call-start = ((), (), s32[]{:S(2)}) async-start(), calls=%async_computation.14 | async-start | bytes 1327104 | tf_op jit(solution)/shard_map/all_gather | solution.py:374
  221.9 106.4 %all-gather.11.cloned.1.call-start = ((), (), s32[]{:S(2)}) async-start(), calls=%async_computation.10 | async-start | bytes 1327104 | tf_op jit(solution)/shard_map/all_gather | solution.py:372
  238.2 1.7 copy-start.9
  238.2 176.6 %reduce-scatter.10.cloned.1.call-start = ((), (), s32[]{:S(2)}) async-start(), calls=%async_computation.7 | async-start | bytes 1216512 | tf_op jit(solution)/shard_map/reduce_scatter | solution.py:393
  239.8 200.0 %all-gather.17.cloned.1.call-start = ((), (), s32[]{:S(2)}) async-start(), calls=%async_computation.13 | async-start | bytes 1327104 | tf_op jit(solution)/shard_map/all_gather | solution.py:416
  444.9 5.2 %copy-start.1 = (bf16[768,768]{1,0:T(8,128)(2,1)S(1)}, bf16[768,768]{1,0:T(8,128)(2,1)}, u32[]{:S(2)}) copy-start(bf16[768,768]{1,0:T(8,128)(2,1)} %param.27) | copy-start | bytes 3538948
  (4 other events, 2.8 us)
Sparse Core Ops, SparseCore 0:
  11.5 61.6 all-gather.12
  75.1 24.6 all-gather.14
  150.9 40.1 reduce-scatter.5
  193.1 21.9 reduce-scatter.11
  217.9 20.2 reduce-scatter.13
  240.9 20.3 reduce-scatter.7
  263.2 23.8 all-gather.18
  289.0 23.7 all-gather.10
  318.4 96.3 reduce-scatter.9
  416.6 23.1 all-gather.16
